TPU v7x, 256 devices: a whole 4x4x8 slice. The times are simulated.
256 devices in a mesh: fluid: 64 (over x, z, core), metal: 4 (over y).
Axes of the slice: x: 4, y: 4, z: 8, core: 2. Of those that a mesh axis runs over, the one named last changes fastest.
Arguments:
- fluid_x: bfloat16 [16384, 512], P('fluid', 'metal'), may hold values from -32 to 32
- metal_x: bfloat16 [8192, 512], P('fluid', 'metal'), may hold values from -32 to 32
- w_rf: bfloat16 [512, 512], P(None, 'metal'), may hold values from -0.5 to 0.5
- w_vf: bfloat16 [512, 512], P(None, 'metal'), may hold values from -0.25 to 0.25
- w_rm: bfloat16 [512, 512], P(None, 'metal'), may hold values from -0.5 to 0.5
- w_vm: bfloat16 [512, 512], P(None, 'metal'), may hold values from -0.25 to 0.25
- fluid_grad: bfloat16 [16384, 512], P('fluid', 'metal'), may hold values from -6 to 6
- metal_grad: bfloat16 [8192, 512], P('fluid', 'metal'), may hold values from -6 to 6
- pair_list: int32 [2048, 2], P('fluid'), may hold values from 0 to 63, as said below
- pair_count: int32 [64], P('fluid'), may hold values from 2 to 32, as said below
Outputs:
- fluid_out: bfloat16 [16384, 512], P('fluid', 'metal')
- metal_out: bfloat16 [8192, 512], P('fluid', 'metal')
- fluid_dx: bfloat16 [16384, 512], P('fluid', 'metal')
- metal_dx: bfloat16 [8192, 512], P('fluid', 'metal')
- weight_grads: float32 [4, 512, 512], P(None, None, 'metal')
Inputs may be any that keep to these rules, and one draw needn't show every extreme that they name: `pair_list`: column 0 is a local fluid block below 2, column 1 a metal block below 64. The first pair_count[d] entries of fluid index d are distinct pairs; every fluid block of every index and every metal block stands in some live entry; entries past the count hold valid indices and are ignored. `pair_count`: some fluid index has all 32 slots live.
All inputs are finite; a program needn't handle non-finite values.
Results may differ from a plain program's by a relative error of at most 0.0179.
The roundings to bfloat16 on the way count: a program that leaves them out, or rounds other values in their place, can miss the bound.
Values may be sent and summed in bfloat16 or wider, within the bound.
No kernel may reach another device: no remote copies, remote signals or barrier semaphores. Data moves between devices by JAX's collectives and lax.ppermute only.
A program may use at most 128 MiB of HBM per device.

v0:
```python
import math
import jax
import jax.numpy as jnp
from jax import lax
from jax.sharding import PartitionSpec as P

D = 512
H = 8
BLK = 128
LOWEST = -1e30


def project(inputs, weight):
    return jnp.dot(inputs, weight, preferred_element_type=jnp.float32).astype(jnp.bfloat16)


def back_project(grads, weight):
    return lax.dot_general(
        grads, weight, (((1,), (1,)), ((), ())), preferred_element_type=jnp.float32
    )


def outer_rows(inputs, grads):
    return lax.dot_general(
        inputs, grads, (((0,), (0,)), ((), ())), preferred_element_type=jnp.float32
    )


def body(fluid_x, metal_x, w_rf, w_vf, w_rm, w_vm, fluid_grad, metal_grad, pair_list, pair_count):
    head_size = D // H
    local_heads = w_rf.shape[1] // head_size
    feature_cols = w_rf.shape[1]
    fluid_rows = fluid_x.shape[0]
    blocks = fluid_rows // BLK
    metal_blocks = lax.axis_size("fluid")
    metal_rows = metal_blocks * BLK
    slot_total = pair_list.shape[0]
    batch_size = math.gcd(slot_total, 16)
    inv_root = 1.0 / math.sqrt(head_size)
    live_count = pair_count[0]
    loop_turns = slot_total // batch_size
    fluid_full, metal_full = (
        lax.all_gather(fluid_x, "metal", axis=1, tiled=True),
        lax.all_gather(metal_x, "metal", axis=1, tiled=True),
    )
    fluid_keys = project(fluid_full, w_rf)
    fluid_values = project(fluid_full, w_vf)
    metal_keys = project(metal_full, w_rm)
    metal_values = project(metal_full, w_vm)
    keys_all, values_all = (
        lax.all_gather(metal_keys, "fluid", axis=0, tiled=True),
        lax.all_gather(metal_values, "fluid", axis=0, tiled=True),
    )
    fkey_tiles = fluid_keys.reshape(blocks, BLK, local_heads, head_size)
    fval_tiles = fluid_values.reshape(blocks, BLK, local_heads, head_size)
    mkey_tiles = keys_all.reshape(metal_blocks, BLK, local_heads, head_size)
    mval_tiles = values_all.reshape(metal_blocks, BLK, local_heads, head_size)

    def batch_pairs(number):
        entries = lax.dynamic_slice_in_dim(pair_list, number * batch_size, batch_size, 0)
        slot_index = number * batch_size + jnp.arange(batch_size, dtype=jnp.int32)
        frows = entries[:, 0]
        mrows = entries[:, 1]
        scores = (
            jnp.einsum(
                "pahd,pbhd->phab",
                fkey_tiles[frows],
                mkey_tiles[mrows],
                preferred_element_type=jnp.float32,
            )
            * inv_root
        )
        return (frows, mrows, slot_index < live_count, scores)

    def max_pass(number, state):
        row_max, col_max = state
        frows, mrows, active, scores = batch_pairs(number)
        live = active[:, None, None]
        row_max = row_max.at[frows].max(jnp.where(live, jnp.max(scores, axis=3), LOWEST))
        col_max = col_max.at[mrows].max(jnp.where(live, jnp.max(scores, axis=2), LOWEST))
        return (row_max, col_max)

    row_max, col_local = lax.fori_loop(
        0,
        loop_turns,
        max_pass,
        (
            jnp.full((blocks, local_heads, BLK), LOWEST, jnp.float32),
            jnp.full((metal_blocks, local_heads, BLK), LOWEST, jnp.float32),
        ),
    )
    col_max = lax.pmax(col_local, "fluid")

    def sum_pass(number, state):
        row_sum, fluid_num, col_sum, metal_num = state
        frows, mrows, active, scores = batch_pairs(number)
        live = active[:, None, None, None]
        row_exp = jnp.where(live, jnp.exp(scores - row_max[frows][:, :, :, None]), 0.0)
        col_exp = jnp.where(live, jnp.exp(scores - col_max[mrows][:, :, None, :]), 0.0)
        row_sum = row_sum.at[frows].add(jnp.sum(row_exp, axis=3))
        col_sum = col_sum.at[mrows].add(jnp.sum(col_exp, axis=2))
        fluid_num = fluid_num.at[frows].add(
            jnp.einsum(
                "phab,pbhd->pahd",
                row_exp.astype(jnp.bfloat16),
                mval_tiles[mrows],
                preferred_element_type=jnp.float32,
            )
        )
        metal_num = metal_num.at[mrows].add(
            jnp.einsum(
                "phab,pahd->pbhd",
                col_exp.astype(jnp.bfloat16),
                fval_tiles[frows],
                preferred_element_type=jnp.float32,
            )
        )
        return (row_sum, fluid_num, col_sum, metal_num)

    row_sum, fluid_num, col_sum, metal_num = lax.fori_loop(
        0,
        loop_turns,
        sum_pass,
        (
            jnp.zeros((blocks, local_heads, BLK), jnp.float32),
            jnp.zeros((blocks, BLK, local_heads, head_size), jnp.float32),
            jnp.zeros((metal_blocks, local_heads, BLK), jnp.float32),
            jnp.zeros((metal_blocks, BLK, local_heads, head_size), jnp.float32),
        ),
    )
    fluid_out = (
        (fluid_num / row_sum.transpose(0, 2, 1)[:, :, :, None])
        .reshape(fluid_rows, feature_cols)
        .astype(jnp.bfloat16)
    )
    num_rows = metal_num.reshape(metal_rows, feature_cols)
    total_rows = col_sum.transpose(0, 2, 1).reshape(metal_rows, local_heads)
    own_num, own_sum = (
        lax.psum_scatter(num_rows, "fluid", scatter_dimension=0, tiled=True),
        lax.psum_scatter(total_rows, "fluid", scatter_dimension=0, tiled=True),
    )
    metal_out = (
        (own_num.reshape(BLK, local_heads, head_size) / own_sum[:, :, None])
        .reshape(BLK, feature_cols)
        .astype(jnp.bfloat16)
    )
    scaled_grad = (
        (metal_grad.astype(jnp.float32).reshape(BLK, local_heads, head_size) / own_sum[:, :, None])
        .reshape(BLK, feature_cols)
        .astype(jnp.bfloat16)
    )
    scaled_all, output_all = (
        lax.all_gather(scaled_grad, "fluid", axis=0, tiled=True),
        lax.all_gather(metal_out, "fluid", axis=0, tiled=True),
    )
    delta_f = jnp.sum(
        (fluid_grad.astype(jnp.float32) * fluid_out.astype(jnp.float32)).reshape(
            fluid_rows, local_heads, head_size
        ),
        axis=2,
    )
    delta_m = jnp.sum(
        (scaled_all.astype(jnp.float32) * output_all.astype(jnp.float32)).reshape(
            metal_blocks, BLK, local_heads, head_size
        ),
        axis=3,
    )
    grad_tiles = fluid_grad.reshape(blocks, BLK, local_heads, head_size)
    scaled_tiles = scaled_all.reshape(metal_blocks, BLK, local_heads, head_size)
    dfluid_tiles = delta_f.reshape(blocks, BLK, local_heads)

    def grad_pass(number, state):
        grad_rf, grad_vf, grad_rm, grad_vm = state
        frows, mrows, active, scores = batch_pairs(number)
        live = active[:, None, None, None]
        attn = jnp.where(
            live,
            jnp.exp(scores - row_max[frows][:, :, :, None]) / row_sum[frows][:, :, :, None],
            0.0,
        )
        col_exp = jnp.where(live, jnp.exp(scores - col_max[mrows][:, :, None, :]), 0.0)
        fluid_term = jnp.einsum(
            "pahd,pbhd->phab",
            grad_tiles[frows],
            mval_tiles[mrows],
            preferred_element_type=jnp.float32,
        )
        metal_term = jnp.einsum(
            "pahd,pbhd->phab",
            fval_tiles[frows],
            scaled_tiles[mrows],
            preferred_element_type=jnp.float32,
        )
        dscore = attn * (fluid_term - dfluid_tiles[frows].transpose(0, 2, 1)[:, :, :, None])
        dscore = dscore + col_exp * (metal_term - delta_m[mrows].transpose(0, 2, 1)[:, :, None, :])
        dscore_weight = dscore.astype(jnp.bfloat16)
        grad_rf = grad_rf.at[frows].add(
            jnp.einsum(
                "phab,pbhd->pahd",
                dscore_weight,
                mkey_tiles[mrows],
                preferred_element_type=jnp.float32,
            )
            * inv_root
        )
        grad_vf = grad_vf.at[frows].add(
            jnp.einsum(
                "phab,pbhd->pahd",
                col_exp.astype(jnp.bfloat16),
                scaled_tiles[mrows],
                preferred_element_type=jnp.float32,
            )
        )
        grad_rm = grad_rm.at[mrows].add(
            jnp.einsum(
                "phab,pahd->pbhd",
                dscore_weight,
                fkey_tiles[frows],
                preferred_element_type=jnp.float32,
            )
            * inv_root
        )
        grad_vm = grad_vm.at[mrows].add(
            jnp.einsum(
                "phab,pahd->pbhd",
                attn.astype(jnp.bfloat16),
                grad_tiles[frows],
                preferred_element_type=jnp.float32,
            )
        )
        return (grad_rf, grad_vf, grad_rm, grad_vm)

    grad_rf, grad_vf, grad_rm, grad_vm = lax.fori_loop(
        0,
        loop_turns,
        grad_pass,
        (
            jnp.zeros((blocks, BLK, local_heads, head_size), jnp.float32),
            jnp.zeros((blocks, BLK, local_heads, head_size), jnp.float32),
            jnp.zeros((metal_blocks, BLK, local_heads, head_size), jnp.float32),
            jnp.zeros((metal_blocks, BLK, local_heads, head_size), jnp.float32),
        ),
    )
    rf_rounded = grad_rf.reshape(fluid_rows, feature_cols).astype(jnp.bfloat16)
    vf_rounded = grad_vf.reshape(fluid_rows, feature_cols).astype(jnp.bfloat16)
    fluid_part = back_project(rf_rounded, w_rf) + back_project(vf_rounded, w_vf)
    fluid_part, weight_rf, weight_vf = (
        fluid_part,
        outer_rows(fluid_full, rf_rounded),
        outer_rows(fluid_full, vf_rounded),
    )
    rm_rounded = lax.psum_scatter(
        grad_rm.reshape(metal_rows, feature_cols), "fluid", scatter_dimension=0, tiled=True
    ).astype(jnp.bfloat16)
    vm_rounded = lax.psum_scatter(
        grad_vm.reshape(metal_rows, feature_cols), "fluid", scatter_dimension=0, tiled=True
    ).astype(jnp.bfloat16)
    metal_part = back_project(rm_rounded, w_rm) + back_project(vm_rounded, w_vm)
    weight_rm = outer_rows(metal_full, rm_rounded)
    weight_vm = outer_rows(metal_full, vm_rounded)
    fluid_dx, metal_dx = (
        lax.psum_scatter(fluid_part, "metal", scatter_dimension=1, tiled=True),
        lax.psum_scatter(metal_part, "metal", scatter_dimension=1, tiled=True),
    )
    weight_grads = lax.psum(jnp.stack([weight_rf, weight_vf, weight_rm, weight_vm]), "fluid")
    return (
        fluid_out,
        metal_out,
        fluid_dx.astype(jnp.bfloat16),
        metal_dx.astype(jnp.bfloat16),
        weight_grads,
    )


def solution(mesh):
    placed = (
        P("fluid", "metal"),
        P("fluid", "metal"),
        P(None, "metal"),
        P(None, "metal"),
        P(None, "metal"),
        P(None, "metal"),
        P("fluid", "metal"),
        P("fluid", "metal"),
        P("fluid", None),
        P("fluid"),
    )
    return jax.shard_map(
        body,
        mesh=mesh,
        in_specs=placed,
        out_specs=(
            P("fluid", "metal"),
            P("fluid", "metal"),
            P("fluid", "metal"),
            P("fluid", "metal"),
            P(None, None, "metal"),
        ),
        check_vma=False,
    )
```

profile of v0, /device:TPU:2, one launch (start us, length us, event | category | flops | bytes accessed | tf_op | source)
XLA Modules:
  0.0 1555.2 jit_solution(13822160661187020611)
XLA Ops:
  7.2 11.8 all_gather.19
  22.6 11.7 all_gather.18
  34.7 64.7 %all-gather.5.cloned.1.call-done = bf16[8192,128]{1,0:T(8,128)(2,1)} async-done(((bf16[128,128]{1,0:T(8,128)(2,1)}), bf16[8192,128]{1,0:T(8,128)(2,1)}) %all-gather.5.cloned.1.call-update) | async-done | bytes 2097168 | tf_op jit(solution)/shard_map/all_gather | solution.py:51
  99.4 8.2 reshape.334
  107.6 23.2 %while.53 = (s32[]{:T(128)}, f32[2,2,128]{2,1,0:T(2,128)S(1)}, f32[64,2,128]{2,1,0:T(2,128)S(1)}, s32[32,2]{0,1:T(2,128)S(1)}, s32[]{:T(128)}, /*index=5*/bf16[2...) while((s32[]{:T(128)}, f32[2,2,128]{2,1,0:T(2,128)S(1)}, ...), condition=%wide.region_5.6_spmd, body=%wide.region_0.5_spmd.sunk | while | flops 68692104 | bytes 3351623 | solution.py:83
  131.9 45.8 %all-gather.7.cloned.1.call-done = bf16[8192,128]{1,0:T(8,128)(2,1)} async-done(((bf16[128,128]{1,0:T(8,128)(2,1)}), bf16[8192,128]{1,0:T(8,128)(2,1)}) %all-gather.7.cloned.1.call-update) | async-done | bytes 2097168 | tf_op jit(solution)/shard_map/all_gather | solution.py:52
  177.7 8.3 reshape.335
  185.9 161.9 %all-reduce.3.cloned.1.call-done = f32[64,2,128]{2,1,0:T(2,128)} async-done(((f32[64,2,128]{2,1,0:T(2,128)}), f32[64,2,128]{2,1,0:T(2,128)}) %all-reduce.3.cloned.1.call-update) | async-done | bytes 65552 | tf_op jit(solution)/shard_map/pmax | solution.py:92
  350.3 67.5 %while.54 = (s32[]{:T(128)}, f32[2,2,128]{2,1,0:T(2,128)S(1)}, f32[2,128,2,64]{1,3,2,0:T(8,128)S(1)}, f32[64,2,128]{2,1,0:T(2,128)S(1)}, f32[64,128,2,64]{1,3,2,...) while((s32[]{:T(128)}, f32[2,2,128]{2,1,0:T(2,128)S(1)}, ...), condition=%wide.region_14.15_spmd, body=%wide.region_7.14_spmd.sunk | while | flops 209717376 | bytes 25437748 | solution.py:120
  358.2 5.7 gather_fusion.4
  391.6 5.7 gather_fusion.4
  431.3 130.0 %reduce-scatter.19.cloned.1.call-done = f32[128,2]{1,0:T(8,128)} async-done(((f32[8192,2]{1,0:T(8,128)}), f32[128,2]{1,0:T(8,128)}) %reduce-scatter.19.cloned.1.call-update) | async-done | bytes 1040
  562.2 145.2 %reduce-scatter.9.cloned.1.call-done = f32[128,128]{0,1:T(8,128)} async-done(((f32[8192,128]{0,1:T(8,128)}), f32[128,128]{0,1:T(8,128)}) %reduce-scatter.9.cloned.1.call-update) | async-done | bytes 65552 | tf_op jit(solution)/shard_map/reduce_scatter | solution.py:139
  710.1 72.3 %all-gather.9.cloned.1.call-done = bf16[8192,128]{0,1:T(8,128)(2,1)} async-done(((bf16[128,128]{0,1:T(8,128)(2,1)}), bf16[8192,128]{0,1:T(8,128)(2,1)}) %all-gather.9.cloned.1.call-update) | async-done | bytes 2097168 | tf_op jit(solution)/shard_map/all_gather | solution.py:153
  782.4 74.9 %all-gather.11.cloned.1.call-done = bf16[8192,128]{0,1:T(8,128)(2,1)} async-done(((bf16[128,128]{0,1:T(8,128)(2,1)}), bf16[8192,128]{0,1:T(8,128)(2,1)}) %all-gather.11.cloned.1.call-update) | async-done | bytes 2097168 | tf_op jit(solution)/shard_map/all_gather | solution.py:154
  877.5 131.7 %while.55 = (s32[]{:T(128)}, f32[2,128,2,64]{1,3,2,0:T(8,128)S(1)}, f32[2,128,2,64]{1,3,2,0:T(8,128)S(1)}, f32[64,128,2,64]{1,3,2,0:T(8,128)}, f32[64,128,2,64]{...) while((s32[]{:T(128)}, f32[2,128,2,64]{1,3,2,0:T(8,128)S(1)}, ...), condition=%wide.region_24.25_spmd, body=%wide.region_19.24_spmd.sunk | while | flops 482347136 | bytes 61189336 | solution.py:233
  895.4 5.7 gather_fusion.8
  961.1 5.7 gather_fusion.8
  1023.8 5.3 copy.185
  1031.5 129.8 %reduce-scatter.15.cloned.1.call-done = f32[128,128]{0,1:T(8,128)} async-done(((f32[8192,128]{0,1:T(8,128)}), f32[128,128]{0,1:T(8,128)}) %reduce-scatter.15.cloned.1.call-update) | async-done | bytes 65552 | tf_op jit(solution)/shard_map/reduce_scatter | solution.py:255
  1162.3 145.3 %reduce-scatter.13.cloned.1.call-done = f32[128,128]{0,1:T(8,128)} async-done(((f32[8192,128]{0,1:T(8,128)}), f32[128,128]{0,1:T(8,128)}) %reduce-scatter.13.cloned.1.call-update) | async-done | bytes 65552 | tf_op jit(solution)/shard_map/reduce_scatter | solution.py:252
  1312.6 20.7 %reduce-scatter.11.cloned.1.call-done = f32[256,128]{1,0:T(8,128)} async-done(((f32[256,512]{1,0:T(8,128)}), f32[256,128]{1,0:T(8,128)}) %reduce-scatter.11.cloned.1.call-update) | async-done | bytes 131088 | tf_op jit(solution)/shard_map/reduce_scatter | solution.py:262
  1334.8 188.6 %all-reduce.5.cloned.1.call-done = f32[4,512,128]{1,2,0:T(8,128)} async-done(((f32[4,512,128]{1,2,0:T(8,128)}), f32[4,512,128]{1,2,0:T(8,128)}) %all-reduce.5.cloned.1.call-update) | async-done | bytes 1048592 | tf_op jit(solution)/shard_map/psum | solution.py:265
  1525.9 20.6 %reduce-scatter.17.cloned.1.call-done = f32[128,128]{1,0:T(8,128)} async-done(((f32[128,512]{1,0:T(8,128)}), f32[128,128]{1,0:T(8,128)}) %reduce-scatter.17.cloned.1.call-update) | async-done | bytes 65552 | tf_op jit(solution)/shard_map/reduce_scatter | solution.py:263
  (269 shorter events, 270.7 us)
Async XLA Ops:
  7.2 27.2 %copy-start = (bf16[512,128]{1,0:T(8,128)(2,1)S(1)}, bf16[512,128]{1,0:T(8,128)(2,1)}, u32[]{:S(2)}) copy-start(bf16[512,128]{1,0:T(8,128)(2,1)} %param.18) | copy-start | bytes 393220
  7.2 92.2 %all-gather.5.cloned.1.call-start = ((), (), s32[]{:S(2)}) async-start(), calls=%async_computation.6 | async-start | bytes 2129920 | tf_op jit(solution)/shard_map/all_gather | solution.py:51
  19.0 15.3 copy-start.8
  20.8 156.9 %all-gather.7.cloned.1.call-start = ((), (), s32[]{:S(2)}) async-start(), calls=%async_computation.7 | async-start | bytes 2129920 | tf_op jit(solution)/shard_map/all_gather | solution.py:52
  22.6 325.3 %all-reduce.3.cloned.1.call-start = ((), (), s32[]{:S(2)}) async-start(), calls=%async_computation.8 | async-start | bytes 131072 | tf_op jit(solution)/shard_map/pmax | solution.py:92
  34.3 97.2 %copy-start.6 = (bf16[256,512]{1,0:T(8,128)(2,1)}, bf16[256,512]{1,0:T(8,128)(2,1)S(1)}, u32[]{:S(2)}) copy-start(bf16[256,512]{1,0:T(8,128)(2,1)S(1)} %all_gather.18) | copy-start | bytes 786436
  34.7 72.9 %copy-start.22 = (s32[32,2]{0,1:T(2,128)S(1)}, s32[32,2]{0,1:T(2,128)}, u32[]{:S(2)}) copy-start(s32[32,2]{0,1:T(2,128)} %param.24) | copy-start | bytes 772
  107.6 24.0 %copy-start.13 = (bf16[512,128]{1,0:T(8,128)(2,1)S(1)}, bf16[512,128]{1,0:T(8,128)(2,1)}, u32[]{:S(2)}) copy-start(bf16[512,128]{1,0:T(8,128)(2,1)} %param.19) | copy-start | bytes 393220
  131.5 429.8 %reduce-scatter.19.cloned.1.call-start = ((), (), s32[]{:S(2)}) async-start(), calls=%async_computation.17 | async-start | bytes 4259840
  410.1 3.9 copy-start.1
  420.5 286.9 %reduce-scatter.9.cloned.1.call-start = ((), (), s32[]{:S(2)}) async-start(), calls=%async_computation.9 | async-start | bytes 4259840 | tf_op jit(solution)/shard_map/reduce_scatter | solution.py:139
  430.4 279.3 %copy-start.20 = (bf16[256,128]{1,0:T(8,128)(2,1)S(1)}, bf16[256,128]{1,0:T(8,128)(2,1)}, u32[]{:S(2)}) copy-start(bf16[256,128]{1,0:T(8,128)(2,1)} %param.22) | copy-start | bytes 196612
  430.5 351.9 %all-gather.9.cloned.1.call-start = ((), (), s32[]{:S(2)}) async-start(), calls=%async_computation.10 | async-start | bytes 2129920 | tf_op jit(solution)/shard_map/all_gather | solution.py:153
  708.9 148.3 %all-gather.11.cloned.1.call-start = ((), (), s32[]{:S(2)}) async-start(), calls=%async_computation.11 | async-start | bytes 2129920 | tf_op jit(solution)/shard_map/all_gather | solution.py:154
  709.7 451.6 %reduce-scatter.15.cloned.1.call-start = ((), (), s32[]{:S(2)}) async-start(), calls=%async_computation.14 | async-start | bytes 4259840 | tf_op jit(solution)/shard_map/reduce_scatter | solution.py:255
  710.0 149.9 %copy-start.11 = (bf16[2,128,2,64]{1,0,3,2:T(2,128)(2,1)}, bf16[2,128,2,64]{1,0,3,2:T(2,128)(2,1)S(1)}, u32[]{:S(2)}) copy-start(bf16[2,128,2,64]{1,0,3,2:T(2,128)(2,1)S(1)} %copy.104) | copy-start | bytes 196612
  1019.1 288.5 %reduce-scatter.13.cloned.1.call-start = ((), (), s32[]{:S(2)}) async-start(), calls=%async_computation.13 | async-start | bytes 4259840 | tf_op jit(solution)/shard_map/reduce_scatter | solution.py:252
  1029.1 304.2 %reduce-scatter.11.cloned.1.call-start = ((), (), s32[]{:S(2)}) async-start(), calls=%async_computation.12 | async-start | bytes 655360 | tf_op jit(solution)/shard_map/reduce_scatter | solution.py:262
  1029.1 132.1 %copy-start.9 = (bf16[128,512]{1,0:T(8,128)(2,1)S(1)}, bf16[128,512]{1,0:T(8,128)(2,1)}, u32[]{:S(2)}) copy-start(bf16[128,512]{1,0:T(8,128)(2,1)} %copy-done.8) | copy-start | bytes 393220
  1031.0 492.3 %all-reduce.5.cloned.1.call-start = ((), (), s32[]{:S(2)}) async-start(), calls=%async_computation.16 | async-start | bytes 2097152 | tf_op jit(solution)/shard_map/psum | solution.py:265
  1031.5 278.4 %copy-start.15 = (bf16[512,128]{1,0:T(8,128)(2,1)S(1)}, bf16[512,128]{1,0:T(8,128)(2,1)}, u32[]{:S(2)}) copy-start(bf16[512,128]{1,0:T(8,128)(2,1)} %param.20) | copy-start | bytes 393220
  1162.3 147.8 %copy-start.16 = (bf16[512,128]{1,0:T(8,128)(2,1)S(1)}, bf16[512,128]{1,0:T(8,128)(2,1)}, u32[]{:S(2)}) copy-start(bf16[512,128]{1,0:T(8,128)(2,1)} %param.21) | copy-start | bytes 393220
  1162.3 147.8 %copy-start.21 = (f32[128,128]{0,1:T(8,128)S(1)}, f32[128,128]{0,1:T(8,128)}, u32[]{:S(2)}) copy-start(f32[128,128]{0,1:T(8,128)} %reduce-scatter.15.cloned.1.call-done) | copy-start | bytes 196612
  1309.8 236.7 %reduce-scatter.17.cloned.1.call-start = ((), (), s32[]{:S(2)}) async-start(), calls=%async_computation.15 | async-start | bytes 327680 | tf_op jit(solution)/shard_map/reduce_scatter | solution.py:263
  (28 other events, 49.7 us)
Sparse Core Ops, SparseCore 0:
  20.9 78.4 all-gather.4
  102.7 74.9 all-gather.6
  181.8 166.0 all-reduce.2
  420.7 140.5 reduce-scatter.18
  565.3 142.0 reduce-scatter.8
  710.7 71.6 all-gather.8
  785.8 71.3 all-gather.10
  1019.2 141.9 reduce-scatter.14
  1165.4 142.1 reduce-scatter.12
  1310.2 23.0 reduce-scatter.10
  1337.7 185.6 all-reduce.4
  1525.7 20.7 reduce-scatter.16
where the time goes:
time: 1570 us; the launch traced here: 1560 us
  waiting for transfers between devices  1200 us (76%)
  local copies, waits for them, and re-layouts  209 us (13%)
  other arithmetic  58.9 us (4%)
  matrix products  46.7 us (3%)
  blocking collectives  23.5 us (1%)
    psum x1, waiting for transfers between devices, body(): lax.psum(jnp.stack([weight_rf, weight_vf, weight_rm, weight_vm]), 'fluid')  189 us
    pmax x1, waiting for transfers between devices, body(): col_max = lax.pmax(col_local, 'fluid')  162 us
    reduce_scatter x1, waiting for transfers between devices, body(): lax.psum_scatter(grad_rm.reshape(metal_rows, feature_cols), 'fluid', scat...  145 us
    reduce_scatter x1, waiting for transfers between devices, body(): lax.psum_scatter(num_rows, 'fluid', scatter_dimension=0, tiled=True)  145 us
    unnamed x13, waiting for transfers between devices  131 us
    reduce_scatter x1, waiting for transfers between devices, body(): lax.psum_scatter(grad_vm.reshape(metal_rows, feature_cols), 'fluid', scat...  130 us
    all_gather x1, waiting for transfers between devices, body(): lax.all_gather(metal_out, 'fluid', axis=0, tiled=True)  74.9 us
    all_gather x1, waiting for transfers between devices, body(): lax.all_gather(scaled_grad, 'fluid', axis=0, tiled=True)  72.3 us
  transfers between devices with their start and end apart: 12, of which 12 were waited for; matrix products, arithmetic and copies ran while one was open for 5% of the time, Pallas kernels for 0%

commit v1 on v0

--- a/solution.py
+++ b/solution.py
@@ -8,6 +8,18 @@
 H = 8
 BLK = 128
 LOWEST = -1e30
+
+
+def collect(x, axis, dim):
+    ways, here, step = (lax.axis_size(axis), lax.axis_index(axis), x.shape[dim])
+    line, have = (x, 1)
+    while have < ways:
+        line = jnp.concatenate(
+            [line, lax.ppermute(line, axis, [(d, (d - have) % ways) for d in range(ways)])],
+            axis=dim,
+        )
+        have = 2 * have
+    return jnp.roll(line, here * step, axis=dim)
 
 
 def project(inputs, weight):
@@ -48,7 +60,7 @@
     metal_keys = project(metal_full, w_rm)
     metal_values = project(metal_full, w_vm)
     keys_all, values_all = (
-        lax.all_gather(metal_keys, "fluid", axis=0, tiled=True),
+        collect(metal_keys, "fluid", 0),
         lax.all_gather(metal_values, "fluid", axis=0, tiled=True),
     )
     fkey_tiles = fluid_keys.reshape(blocks, BLK, local_heads, head_size)

time: 1570 us -> 1540 us (0.981)
  waiting for transfers between devices: 1200 us -> 1160 us
    all_gather x1 -> x0, waiting for transfers between devices: 64.7 us -> none  [body(): lax.all_gather(metal_keys, 'fluid', axis=0, tiled=True)]
    ppermute x0 -> x6, waiting for transfers between devices: none -> 44.7 us  [collect(): lax.ppermute(line, axis, [(d, (d - have) % ways) for d in range(ways)])]
    all_gather x1, waiting for transfers between devices: 45.8 us -> 23.5 us  [body(): lax.all_gather(metal_values, 'fluid', axis=0, tiled=True)]
    unnamed x49 -> x66, local copies, waits for them, and re-layouts: 30.1 us -> 38.4 us
    unnamed x13 -> x12, waiting for transfers between devices: 131 us -> 131 us
  transfers between devices with their start and end apart: 12 -> 17, of which waited for: 12 -> 17; matrix products, arithmetic and copies ran while one was open for 5% -> 5% of each run, Pallas kernels for 0% -> 0%
where the time goes in v1:
time: 1540 us; the launch traced here: 1530 us
  waiting for transfers between devices  1160 us (75%)
  local copies, waits for them, and re-layouts  216 us (14%)
  other arithmetic  59 us (4%)
  matrix products  44.9 us (3%)
  blocking collectives  24.2 us (2%)
    psum x1, waiting for transfers between devices, body(): lax.psum(jnp.stack([weight_rf, weight_vf, weight_rm, weight_vm]), 'fluid')  188 us
    pmax x1, waiting for transfers between devices, body(): col_max = lax.pmax(col_local, 'fluid')  162 us
    reduce_scatter x1, waiting for transfers between devices, body(): lax.psum_scatter(grad_rm.reshape(metal_rows, feature_cols), 'fluid', scat...  145 us
    reduce_scatter x1, waiting for transfers between devices, body(): lax.psum_scatter(num_rows, 'fluid', scatter_dimension=0, tiled=True)  145 us
    unnamed x12, waiting for transfers between devices  131 us
    reduce_scatter x1, waiting for transfers between devices, body(): lax.psum_scatter(grad_vm.reshape(metal_rows, feature_cols), 'fluid', scat...  129 us
    all_gather x1, waiting for transfers between devices, body(): lax.all_gather(metal_out, 'fluid', axis=0, tiled=True)  74.7 us
    all_gather x1, waiting for transfers between devices, body(): lax.all_gather(scaled_grad, 'fluid', axis=0, tiled=True)  72.4 us
  transfers between devices with their start and end apart: 17, of which 17 were waited for; matrix products, arithmetic and copies ran while one was open for 5% of the time, Pallas kernels for 0%

profile of v1, /device:TPU:2, one launch (start us, length us, event | category | flops | bytes accessed | tf_op | source)
XLA Modules:
  0.0 1531.7 jit_solution(14994831264107501151)
XLA Ops:
  7.2 11.8 all_gather.16
  44.9 11.1 collective-permute-done.3
  56.8 12.9 collective-permute-done.4
  71.7 12.4 all_gather.15
  84.4 11.5 collective-permute-done.5
  107.1 23.2 %while.53 = (s32[]{:T(128)}, f32[2,2,128]{2,1,0:T(2,128)S(1)}, f32[64,2,128]{2,1,0:T(2,128)S(1)}, s32[32,2]{0,1:T(2,128)S(1)}, s32[]{:T(128)}, /*index=5*/bf16[2...) while((s32[]{:T(128)}, f32[2,2,128]{2,1,0:T(2,128)S(1)}, ...), condition=%wide.region_5.6_spmd, body=%wide.region_0.5_spmd.sunk | while | flops 68692104 | bytes 3351623 | solution.py:95
  131.4 23.5 %all-gather.4.cloned.1.call-done = bf16[8192,128]{1,0:T(8,128)(2,1)} async-done(((bf16[128,128]{1,0:T(8,128)(2,1)}), bf16[8192,128]{1,0:T(8,128)(2,1)}) %all-gather.4.cloned.1.call-update) | async-done | bytes 2097168 | tf_op jit(solution)/shard_map/all_gather | solution.py:64
  155.0 8.3 reshape.335
  163.2 161.8 %all-reduce.3.cloned.1.call-done = f32[64,2,128]{2,1,0:T(2,128)} async-done(((f32[64,2,128]{2,1,0:T(2,128)}), f32[64,2,128]{2,1,0:T(2,128)}) %all-reduce.3.cloned.1.call-update) | async-done | bytes 65552 | tf_op jit(solution)/shard_map/pmax | solution.py:104
  327.5 67.4 %while.54 = (s32[]{:T(128)}, f32[2,2,128]{2,1,0:T(2,128)S(1)}, f32[2,128,2,64]{1,3,2,0:T(8,128)S(1)}, f32[64,2,128]{2,1,0:T(2,128)S(1)}, f32[64,128,2,64]{1,3,2,...) while((s32[]{:T(128)}, f32[2,2,128]{2,1,0:T(2,128)S(1)}, ...), condition=%wide.region_14.15_spmd, body=%wide.region_7.14_spmd.sunk | while | flops 209717376 | bytes 25437748 | solution.py:132
  335.3 5.7 gather_fusion.4
  368.7 5.7 gather_fusion.4
  408.4 130.0 %reduce-scatter.19.cloned.1.call-done = f32[128,2]{1,0:T(8,128)} async-done(((f32[8192,2]{1,0:T(8,128)}), f32[128,2]{1,0:T(8,128)}) %reduce-scatter.19.cloned.1.call-update) | async-done | bytes 1040
  539.3 145.3 %reduce-scatter.9.cloned.1.call-done = f32[128,128]{0,1:T(8,128)} async-done(((f32[8192,128]{0,1:T(8,128)}), f32[128,128]{0,1:T(8,128)}) %reduce-scatter.9.cloned.1.call-update) | async-done | bytes 65552 | tf_op jit(solution)/shard_map/reduce_scatter | solution.py:151
  687.1 72.4 %all-gather.6.cloned.1.call-done = bf16[8192,128]{0,1:T(8,128)(2,1)} async-done(((bf16[128,128]{0,1:T(8,128)(2,1)}), bf16[8192,128]{0,1:T(8,128)(2,1)}) %all-gather.6.cloned.1.call-update) | async-done | bytes 2097168 | tf_op jit(solution)/shard_map/all_gather | solution.py:165
  759.6 74.7 %all-gather.8.cloned.1.call-done = bf16[8192,128]{0,1:T(8,128)(2,1)} async-done(((bf16[128,128]{0,1:T(8,128)(2,1)}), bf16[8192,128]{0,1:T(8,128)(2,1)}) %all-gather.8.cloned.1.call-update) | async-done | bytes 2097168 | tf_op jit(solution)/shard_map/all_gather | solution.py:166
  854.5 131.8 %while.55 = (s32[]{:T(128)}, f32[2,128,2,64]{1,3,2,0:T(8,128)S(1)}, f32[2,128,2,64]{1,3,2,0:T(8,128)S(1)}, f32[64,128,2,64]{1,3,2,0:T(8,128)}, f32[64,128,2,64]{...) while((s32[]{:T(128)}, f32[2,128,2,64]{1,3,2,0:T(8,128)S(1)}, ...), condition=%wide.region_24.25_spmd, body=%wide.region_19.24_spmd.sunk | while | flops 482347136 | bytes 61189336 | solution.py:245
  872.4 5.7 gather_fusion.8
  938.1 5.7 gather_fusion.8
  1008.8 129.5 %reduce-scatter.15.cloned.1.call-done = f32[128,128]{0,1:T(8,128)} async-done(((f32[8192,128]{0,1:T(8,128)}), f32[128,128]{0,1:T(8,128)}) %reduce-scatter.15.cloned.1.call-update) | async-done | bytes 65552 | tf_op jit(solution)/shard_map/reduce_scatter | solution.py:267
  1139.4 145.4 %reduce-scatter.13.cloned.1.call-done = f32[128,128]{0,1:T(8,128)} async-done(((f32[8192,128]{0,1:T(8,128)}), f32[128,128]{0,1:T(8,128)}) %reduce-scatter.13.cloned.1.call-update) | async-done | bytes 65552 | tf_op jit(solution)/shard_map/reduce_scatter | solution.py:264
  1289.7 21.0 %reduce-scatter.11.cloned.1.call-done = f32[256,128]{1,0:T(8,128)} async-done(((f32[256,512]{1,0:T(8,128)}), f32[256,128]{1,0:T(8,128)}) %reduce-scatter.11.cloned.1.call-update) | async-done | bytes 131088 | tf_op jit(solution)/shard_map/reduce_scatter | solution.py:274
  1312.2 187.8 %all-reduce.5.cloned.1.call-done = f32[4,512,128]{1,2,0:T(8,128)} async-done(((f32[4,512,128]{1,2,0:T(8,128)}), f32[4,512,128]{1,2,0:T(8,128)}) %all-reduce.5.cloned.1.call-update) | async-done | bytes 1048592 | tf_op jit(solution)/shard_map/psum | solution.py:277
  1502.6 20.8 %reduce-scatter.17.cloned.1.call-done = f32[128,128]{1,0:T(8,128)} async-done(((f32[128,512]{1,0:T(8,128)}), f32[128,128]{1,0:T(8,128)}) %reduce-scatter.17.cloned.1.call-update) | async-done | bytes 65552 | tf_op jit(solution)/shard_map/reduce_scatter | solution.py:275
  (301 shorter events, 312.3 us)
Async XLA Ops:
  7.2 147.8 %all-gather.4.cloned.1.call-start = ((), (), s32[]{:S(2)}) async-start(), calls=%async_computation.6 | async-start | bytes 2129920 | tf_op jit(solution)/shard_map/all_gather | solution.py:64
  19.0 51.7 %copy-start.8 = (bf16[128,512]{1,0:T(8,128)(2,1)}, bf16[128,512]{1,0:T(8,128)(2,1)S(1)}, u32[]{:S(2)}) copy-start(bf16[128,512]{1,0:T(8,128)(2,1)S(1)} %all_gather.16) | copy-start | bytes 393220
  19.8 4.5 collective-permute-start
  24.4 5.1 collective-permute-start.1
  29.5 8.6 collective-permute-start.2
  38.1 17.8 %collective-permute-start.3 = (bf16[1024,128]{1,0:T(8,128)(2,1)S(1)}, bf16[1024,128]{1,0:T(8,128)(2,1)S(1)}, u32[]{:S(2)}, u32[]{:S(2)}) collective-permute-start(bf16[1024,128]{1,0:T(8,128)(2,1)S(1)} %pad_maximum_fusion.1), channel_id=1, source_target_pairs={{0,224},{4,228},{8,232},{12,236},{16,240},{20,244},{24,248},{28,25... | collective-permute-start | bytes 786440 | tf_op jit(solution)/shard_map/ppermute | solution.py:18
  56.8 12.9 collective-permute-start.4
  70.8 25.1 %collective-permute-start.5 = (bf16[4096,128]{1,0:T(8,128)(2,1)}, bf16[4096,128]{1,0:T(8,128)(2,1)S(1)}, u32[]{:S(2)}, u32[]{:S(2)}) collective-permute-start(bf16[4096,128]{1,0:T(8,128)(2,1)} %get-tuple-element.835), channel_id=1, source_target_pairs={{0,128},{4,132},{8,136},{12,140},{16,144},{20,148},{24,152},{28,15... | collective-permute-start | bytes 3145736 | tf_op jit(solution)/shard_map/ppermute | solution.py:18
  71.6 253.4 %all-reduce.3.cloned.1.call-start = ((), (), s32[]{:S(2)}) async-start(), calls=%async_computation.7 | async-start | bytes 131072 | tf_op jit(solution)/shard_map/pmax | solution.py:104
  84.0 47.1 %copy-start.6 = (bf16[256,512]{1,0:T(8,128)(2,1)}, bf16[256,512]{1,0:T(8,128)(2,1)S(1)}, u32[]{:S(2)}) copy-start(bf16[256,512]{1,0:T(8,128)(2,1)S(1)} %all_gather.15) | copy-start | bytes 786436
  131.1 407.3 %reduce-scatter.19.cloned.1.call-start = ((), (), s32[]{:S(2)}) async-start(), calls=%async_computation.16 | async-start | bytes 4259840
  397.6 287.0 %reduce-scatter.9.cloned.1.call-start = ((), (), s32[]{:S(2)}) async-start(), calls=%async_computation.8 | async-start | bytes 4259840 | tf_op jit(solution)/shard_map/reduce_scatter | solution.py:151
  407.5 279.3 %copy-start.22 = (bf16[256,128]{1,0:T(8,128)(2,1)S(1)}, bf16[256,128]{1,0:T(8,128)(2,1)}, u32[]{:S(2)}) copy-start(bf16[256,128]{1,0:T(8,128)(2,1)} %param.22) | copy-start | bytes 196612
  407.5 352.0 %all-gather.6.cloned.1.call-start = ((), (), s32[]{:S(2)}) async-start(), calls=%async_computation.9 | async-start | bytes 2129920 | tf_op jit(solution)/shard_map/all_gather | solution.py:165
  686.1 148.1 %all-gather.8.cloned.1.call-start = ((), (), s32[]{:S(2)}) async-start(), calls=%async_computation.10 | async-start | bytes 2129920 | tf_op jit(solution)/shard_map/all_gather | solution.py:166
  686.7 451.6 %reduce-scatter.15.cloned.1.call-start = ((), (), s32[]{:S(2)}) async-start(), calls=%async_computation.13 | async-start | bytes 4259840 | tf_op jit(solution)/shard_map/reduce_scatter | solution.py:267
  687.1 149.9 %copy-start.11 = (bf16[2,128,2,64]{1,0,3,2:T(2,128)(2,1)}, bf16[2,128,2,64]{1,0,3,2:T(2,128)(2,1)S(1)}, u32[]{:S(2)}) copy-start(bf16[2,128,2,64]{1,0,3,2:T(2,128)(2,1)S(1)} %copy.104) | copy-start | bytes 196612
  996.2 288.5 %reduce-scatter.13.cloned.1.call-start = ((), (), s32[]{:S(2)}) async-start(), calls=%async_computation.12 | async-start | bytes 4259840 | tf_op jit(solution)/shard_map/reduce_scatter | solution.py:264
  1006.2 304.5 %reduce-scatter.11.cloned.1.call-start = ((), (), s32[]{:S(2)}) async-start(), calls=%async_computation.11 | async-start | bytes 655360 | tf_op jit(solution)/shard_map/reduce_scatter | solution.py:274
  1006.2 132.1 %copy-start.9 = (bf16[128,512]{1,0:T(8,128)(2,1)S(1)}, bf16[128,512]{1,0:T(8,128)(2,1)}, u32[]{:S(2)}) copy-start(bf16[128,512]{1,0:T(8,128)(2,1)} %copy-done.8) | copy-start | bytes 393220
  1008.4 491.6 %all-reduce.5.cloned.1.call-start = ((), (), s32[]{:S(2)}) async-start(), calls=%async_computation.15 | async-start | bytes 2097152 | tf_op jit(solution)/shard_map/psum | solution.py:277
  1139.3 147.9 %copy-start.18 = (bf16[512,128]{1,0:T(8,128)(2,1)S(1)}, bf16[512,128]{1,0:T(8,128)(2,1)}, u32[]{:S(2)}) copy-start(bf16[512,128]{1,0:T(8,128)(2,1)} %param.21) | copy-start | bytes 393220
  1139.3 147.9 %copy-start.23 = (f32[128,128]{0,1:T(8,128)S(1)}, f32[128,128]{0,1:T(8,128)}, u32[]{:S(2)}) copy-start(f32[128,128]{0,1:T(8,128)} %reduce-scatter.15.cloned.1.call-done) | copy-start | bytes 196612
  1286.9 236.4 %reduce-scatter.17.cloned.1.call-start = ((), (), s32[]{:S(2)}) async-start(), calls=%async_computation.14 | async-start | bytes 327680 | tf_op jit(solution)/shard_map/reduce_scatter | solution.py:275
  (36 other events, 209.5 us)
Sparse Core Ops, SparseCore 0:
  71.7 83.2 all-gather.3
  159.0 165.9 all-reduce.2
  397.7 140.6 reduce-scatter.18
  542.4 142.2 reduce-scatter.8
  687.9 71.5 all-gather.5
  762.9 71.3 all-gather.7
  996.3 141.9 reduce-scatter.14
  1142.4 142.2 reduce-scatter.12
  1287.4 23.1 reduce-scatter.10
  1314.9 185.1 all-reduce.4
  1502.6 20.7 reduce-scatter.16
